TPU v7x, 768 devices: a whole 4x8x12 slice. The times are simulated.
768 devices in a mesh: row: 12 (over z), col: 64 (over x, y, core).
Axes of the slice: x: 4, y: 8, z: 12, core: 2. Of those that a mesh axis runs over, the one named last changes fastest.
Arguments:
- x_band: float32 [4608, 64, 448], P(('row', 'col')), may hold values from -0.25 to 0.25
- x_mask: int32 [4608, 7], P(('row', 'col')), may hold values 0 or 1
- g_mask: int32 [4608, 7], P(('row', 'col')), may hold values 0 or 1
Outputs:
- z_band: float32 [4608, 64, 448], P(('row', 'col'))
All inputs are finite; a program needn't handle non-finite values. No bound on the sum of `x_mask` or of `g_mask` on one device may be relied on, other than what follows from the above.
Results may differ from a plain program's by a relative error of at most 0.0001.
Values sent between devices are 32-bit elements; how exact they have to be, the bound alone decides.
A program may use at most 64 MiB of HBM per device.

v0:
```python
import jax
import jax.numpy as jnp
from jax import lax
from jax.sharding import PartitionSpec as P

BS = 64
HALF = 3
W = 7


def with_halo(cells, sides, width):
    for axis, dim in sides:
        count = lax.axis_size(axis)
        head = lax.slice_in_dim(cells, 0, width, axis=dim)
        tail = lax.slice_in_dim(cells, cells.shape[dim] - width, cells.shape[dim], axis=dim)
        cells = jnp.concatenate(
            [
                lax.ppermute(tail, axis, [(i, (i + 1) % count) for i in range(count)]),
                cells,
                lax.ppermute(head, axis, [((i + 1) % count, i) for i in range(count)]),
            ],
            axis=dim,
        )
    return cells


def band_mult(left_band, haloed):
    row_count = left_band.shape[0]
    band_len = left_band.shape[2]
    padded = jnp.pad(haloed, ((0, 0), (0, 0), (HALF, HALF), (0, 0)))

    def advance(running, offset):
        near_rows = lax.dynamic_slice_in_dim(padded, offset, row_count, 0)
        window = lax.dynamic_slice_in_dim(near_rows, 2 * HALF - offset, band_len, 2)
        left_block = lax.dynamic_index_in_dim(left_band, offset, 2, keepdims=False)
        term = jnp.einsum("iac,icub->iaub", left_block, window, precision=lax.Precision.HIGHEST)
        return (running + term, None)

    zero_sum = jnp.zeros(left_band.shape, jnp.float32)
    running, _ = lax.scan(advance, zero_sum, jnp.arange(band_len, dtype=jnp.int32))
    return running


def near_rim(field):
    return with_halo(field, ((("row", "col"), 0),), HALF)


def body(x_band, x_mask, g_mask):
    row_count = x_band.shape[0]
    blocks = x_band.reshape(row_count, BS, W, BS)
    pattern = x_mask.astype(jnp.float32)[:, None, :, None]
    matrix_x = blocks * pattern
    g_pattern = g_mask.astype(jnp.float32)[:, None, :, None]
    square = band_mult(matrix_x, near_rim(matrix_x)) * g_pattern
    cubic_term = band_mult(matrix_x, near_rim(square))
    result = (1.5 * matrix_x - 0.5 * cubic_term) * pattern
    return result.reshape(row_count, BS, W * BS)


def solution(mesh):
    placed = (P(("row", "col"), None, None), P(("row", "col"), None), P(("row", "col"), None))
    return jax.shard_map(
        body, mesh=mesh, in_specs=placed, out_specs=P(("row", "col"), None, None), check_vma=False
    )
```

profile of v0, /device:TPU:255, one launch (start us, length us, event | category | flops | bytes accessed | tf_op | source)
XLA Modules:
  0.0 178.5 jit_solution(11184645556397529873)
XLA Ops:
  0.0 2.7 %reshape.8 = f32[6,64,7,64]{3,2,1,0:T(8,128)} reshape(f32[6,64,448]{2,1,0:T(8,128)} %param.7) | data formatting | bytes 1376256 | tf_op jit(solution)/shard_map/reshape | solution.py:50
  5.3 4.9 %collective-permute-start = (f32[3,64,7,64]{3,1,2,0:T(8,128)}, f32[3,64,7,64]{3,1,2,0:T(8,128)}, u32[]{:S(2)}, u32[]{:S(2)}) collective-permute-start(f32[3,64,7,64]{3,1,2,0:T(8,128)} %copy.11), channel_id=1, source_target_pairs={{0,1},{1,2},{2,3},{3,4},{4,5},{5,6},{6,7},{7,8},{8,9},{9,10},{10,1... | collective-permute-start | bytes 1032200 | tf_op jit(solution)/shard_map/ppermute | solution.py:18
  14.6 3.8 %collective-permute-done = f32[3,64,7,64]{3,1,2,0:T(8,128)} collective-permute-done((f32[3,64,7,64]{3,1,2,0:T(8,128)}, f32[3,64,7,64]{3,1,2,0:T(8,128)}, u32[]{:S(2)}, u32[]{:S(2)}) %collective-permute-start) | collective-permute-done | bytes 344096 | tf_op jit(solution)/shard_map/ppermute | solution.py:18
  19.9 9.4 %collective-permute-done.1 = f32[3,64,7,64]{3,1,2,0:T(8,128)} collective-permute-done((f32[3,64,7,64]{3,1,2,0:T(8,128)}, f32[3,64,7,64]{3,1,2,0:T(8,128)}, u32[]{:S(2)}, u32[]{:S(2)}) %collective-permute-start.1) | collective-permute-done | bytes 344096 | tf_op jit(solution)/shard_map/ppermute | solution.py:20
  31.7 3.0 %pad.7.clone = f32[12,64,13,64]{3,1,2,0:T(8,128)} pad(f32[12,64,7,64]{3,1,2,0:T(8,128)S(1)} %copy.21, f32[]{:T(128)} %constant.161.clone.1), padding=0_0x0_0x3_3x0_0 | pad | bytes 3932164 | tf_op jit(solution)/shard_map/jit(_pad)/pad | solution.py:30
  34.8 57.3 %while.28 = (s32[]{:T(128)}, f32[6,64,7,64]{3,1,2,0:T(8,128)S(1)}, s32[7]{0:T(128)S(1)}, f32[6,64,7,64]{3,1,0,2:T(8,128)}, f32[12,64,13,64]{3,1,2,0:T(8,128)}, /...) while((s32[]{:T(128)}, f32[6,64,7,64]{3,1,2,0:T(8,128)S(1)}, ...), condition=%wide.region_1.2_spmd.clone, body=%wide.region_0.1_spmd.clone.sunk | while | flops 132464656 | bytes 2949400 | solution.py:40
  39.9 3.0 %convolution_add_fusion.4 = f32[6,64,7,64]{3,1,2,0:T(8,128)S(1)} fusion(f32[6,64,7,64]{3,1,2,0:T(8,128)S(1)} %get-tuple-element.339, f32[12,64,13,64]{3,1,2,0:T(8,128)} %get-tuple-element.353, s32[]{:T(128)S(6)} %select_n.72, s32[]{:T(128)S(6)} %select_n.74, pred[]{:T(512)S(6)} %compare.22, f32[6,64,7,64]{3,1,0,2:T(8,128)} %get-tuple-element.352, ...), kind=kOutput, calls=%fused_computation.clone.1 | convolution fusion | flops 132464640 | bytes 2949133 | tf_op jit(solution)/shard_map/while/body/eval_jaxpr/iac,icub->iaub/dot_general | solution.py:36
  48.1 3.0 %convolution_add_fusion.4 = f32[6,64,7,64]{3,1,2,0:T(8,128)S(1)} fusion(f32[6,64,7,64]{3,1,2,0:T(8,128)S(1)} %get-tuple-element.339, f32[12,64,13,64]{3,1,2,0:T(8,128)} %get-tuple-element.353, s32[]{:T(128)S(6)} %select_n.72, s32[]{:T(128)S(6)} %select_n.74, pred[]{:T(512)S(6)} %compare.22, f32[6,64,7,64]{3,1,0,2:T(8,128)} %get-tuple-element.352, ...), kind=kOutput, calls=%fused_computation.clone.1 | convolution fusion | flops 132464640 | bytes 2949133 | tf_op jit(solution)/shard_map/while/body/eval_jaxpr/iac,icub->iaub/dot_general | solution.py:36
  56.2 3.0 %convolution_add_fusion.4 = f32[6,64,7,64]{3,1,2,0:T(8,128)S(1)} fusion(f32[6,64,7,64]{3,1,2,0:T(8,128)S(1)} %get-tuple-element.339, f32[12,64,13,64]{3,1,2,0:T(8,128)} %get-tuple-element.353, s32[]{:T(128)S(6)} %select_n.72, s32[]{:T(128)S(6)} %select_n.74, pred[]{:T(512)S(6)} %compare.22, f32[6,64,7,64]{3,1,0,2:T(8,128)} %get-tuple-element.352, ...), kind=kOutput, calls=%fused_computation.clone.1 | convolution fusion | flops 132464640 | bytes 2949133 | tf_op jit(solution)/shard_map/while/body/eval_jaxpr/iac,icub->iaub/dot_general | solution.py:36
  64.4 3.0 %convolution_add_fusion.4 = f32[6,64,7,64]{3,1,2,0:T(8,128)S(1)} fusion(f32[6,64,7,64]{3,1,2,0:T(8,128)S(1)} %get-tuple-element.339, f32[12,64,13,64]{3,1,2,0:T(8,128)} %get-tuple-element.353, s32[]{:T(128)S(6)} %select_n.72, s32[]{:T(128)S(6)} %select_n.74, pred[]{:T(512)S(6)} %compare.22, f32[6,64,7,64]{3,1,0,2:T(8,128)} %get-tuple-element.352, ...), kind=kOutput, calls=%fused_computation.clone.1 | convolution fusion | flops 132464640 | bytes 2949133 | tf_op jit(solution)/shard_map/while/body/eval_jaxpr/iac,icub->iaub/dot_general | solution.py:36
  72.6 3.0 %convolution_add_fusion.4 = f32[6,64,7,64]{3,1,2,0:T(8,128)S(1)} fusion(f32[6,64,7,64]{3,1,2,0:T(8,128)S(1)} %get-tuple-element.339, f32[12,64,13,64]{3,1,2,0:T(8,128)} %get-tuple-element.353, s32[]{:T(128)S(6)} %select_n.72, s32[]{:T(128)S(6)} %select_n.74, pred[]{:T(512)S(6)} %compare.22, f32[6,64,7,64]{3,1,0,2:T(8,128)} %get-tuple-element.352, ...), kind=kOutput, calls=%fused_computation.clone.1 | convolution fusion | flops 132464640 | bytes 2949133 | tf_op jit(solution)/shard_map/while/body/eval_jaxpr/iac,icub->iaub/dot_general | solution.py:36
  80.8 3.0 %convolution_add_fusion.4 = f32[6,64,7,64]{3,1,2,0:T(8,128)S(1)} fusion(f32[6,64,7,64]{3,1,2,0:T(8,128)S(1)} %get-tuple-element.339, f32[12,64,13,64]{3,1,2,0:T(8,128)} %get-tuple-element.353, s32[]{:T(128)S(6)} %select_n.72, s32[]{:T(128)S(6)} %select_n.74, pred[]{:T(512)S(6)} %compare.22, f32[6,64,7,64]{3,1,0,2:T(8,128)} %get-tuple-element.352, ...), kind=kOutput, calls=%fused_computation.clone.1 | convolution fusion | flops 132464640 | bytes 2949133 | tf_op jit(solution)/shard_map/while/body/eval_jaxpr/iac,icub->iaub/dot_general | solution.py:36
  89.0 3.0 %convolution_add_fusion.4 = f32[6,64,7,64]{3,1,2,0:T(8,128)S(1)} fusion(f32[6,64,7,64]{3,1,2,0:T(8,128)S(1)} %get-tuple-element.339, f32[12,64,13,64]{3,1,2,0:T(8,128)} %get-tuple-element.353, s32[]{:T(128)S(6)} %select_n.72, s32[]{:T(128)S(6)} %select_n.74, pred[]{:T(512)S(6)} %compare.22, f32[6,64,7,64]{3,1,0,2:T(8,128)} %get-tuple-element.352, ...), kind=kOutput, calls=%fused_computation.clone.1 | convolution fusion | flops 132464640 | bytes 2949133 | tf_op jit(solution)/shard_map/while/body/eval_jaxpr/iac,icub->iaub/dot_general | solution.py:36
  97.5 5.8 %collective-permute-done.2 = f32[3,64,7,64]{3,1,2,0:T(8,128)} collective-permute-done((f32[3,64,7,64]{3,1,2,0:T(8,128)}, f32[3,64,7,64]{3,1,2,0:T(8,128)}, u32[]{:S(2)}, u32[]{:S(2)}) %collective-permute-start.2) | collective-permute-done | bytes 344096 | tf_op jit(solution)/shard_map/ppermute | solution.py:18
  103.3 9.6 %collective-permute-done.3 = f32[3,64,7,64]{3,1,2,0:T(8,128)} collective-permute-done((f32[3,64,7,64]{3,1,2,0:T(8,128)S(1)}, f32[3,64,7,64]{3,1,2,0:T(8,128)}, u32[]{:S(2)}, u32[]{:S(2)}) %collective-permute-start.3) | collective-permute-done | bytes 344096 | tf_op jit(solution)/shard_map/ppermute | solution.py:20
  112.9 3.7 %select_maximum_fusion = f32[12,64,13,64]{3,1,2,0:T(8,128)} fusion(f32[3,64,7,64]{3,1,2,0:T(8,128)} %collective-permute-done.3, f32[6,64,7,64]{3,1,2,0:T(8,128)S(1)} %broadcast_multiply_fusion.1, f32[3,64,7,64]{3,1,2,0:T(8,128)} %collective-permute-done.2), kind=kLoop, calls=%fused_computation.12 | loop fusion | flops 5111808 | bytes 3932160 | tf_op jit(solution)/shard_map/concatenate | solution.py:16
  116.6 57.3 %while.29 = (s32[]{:T(128)}, f32[6,64,7,64]{3,1,2,0:T(8,128)S(1)}, s32[7]{0:T(128)S(1)}, f32[6,64,7,64]{3,1,0,2:T(8,128)}, f32[12,64,13,64]{3,1,2,0:T(8,128)}, /...) while((s32[]{:T(128)}, f32[6,64,7,64]{3,1,2,0:T(8,128)S(1)}, ...), condition=%wide.region_3.4_spmd.clone, body=%wide.region_2.3_spmd.clone.sunk | while | flops 132464656 | bytes 2949400 | solution.py:40
  121.7 3.0 %convolution_add_fusion.5 = f32[6,64,7,64]{3,1,2,0:T(8,128)S(1)} fusion(f32[6,64,7,64]{3,1,2,0:T(8,128)S(1)} %get-tuple-element.372, f32[12,64,13,64]{3,1,2,0:T(8,128)} %get-tuple-element.386, s32[]{:T(128)S(6)} %select_n.77, s32[]{:T(128)S(6)} %select_n.79, pred[]{:T(512)S(6)} %compare.23, f32[6,64,7,64]{3,1,0,2:T(8,128)} %get-tuple-element.385, ...), kind=kOutput, calls=%fused_computation.5.clone.1 | convolution fusion | flops 132464640 | bytes 2949133 | tf_op jit(solution)/shard_map/while/body/eval_jaxpr/iac,icub->iaub/dot_general | solution.py:36
  129.9 3.0 %convolution_add_fusion.5 = f32[6,64,7,64]{3,1,2,0:T(8,128)S(1)} fusion(f32[6,64,7,64]{3,1,2,0:T(8,128)S(1)} %get-tuple-element.372, f32[12,64,13,64]{3,1,2,0:T(8,128)} %get-tuple-element.386, s32[]{:T(128)S(6)} %select_n.77, s32[]{:T(128)S(6)} %select_n.79, pred[]{:T(512)S(6)} %compare.23, f32[6,64,7,64]{3,1,0,2:T(8,128)} %get-tuple-element.385, ...), kind=kOutput, calls=%fused_computation.5.clone.1 | convolution fusion | flops 132464640 | bytes 2949133 | tf_op jit(solution)/shard_map/while/body/eval_jaxpr/iac,icub->iaub/dot_general | solution.py:36
  138.1 3.0 %convolution_add_fusion.5 = f32[6,64,7,64]{3,1,2,0:T(8,128)S(1)} fusion(f32[6,64,7,64]{3,1,2,0:T(8,128)S(1)} %get-tuple-element.372, f32[12,64,13,64]{3,1,2,0:T(8,128)} %get-tuple-element.386, s32[]{:T(128)S(6)} %select_n.77, s32[]{:T(128)S(6)} %select_n.79, pred[]{:T(512)S(6)} %compare.23, f32[6,64,7,64]{3,1,0,2:T(8,128)} %get-tuple-element.385, ...), kind=kOutput, calls=%fused_computation.5.clone.1 | convolution fusion | flops 132464640 | bytes 2949133 | tf_op jit(solution)/shard_map/while/body/eval_jaxpr/iac,icub->iaub/dot_general | solution.py:36
  146.2 3.0 %convolution_add_fusion.5 = f32[6,64,7,64]{3,1,2,0:T(8,128)S(1)} fusion(f32[6,64,7,64]{3,1,2,0:T(8,128)S(1)} %get-tuple-element.372, f32[12,64,13,64]{3,1,2,0:T(8,128)} %get-tuple-element.386, s32[]{:T(128)S(6)} %select_n.77, s32[]{:T(128)S(6)} %select_n.79, pred[]{:T(512)S(6)} %compare.23, f32[6,64,7,64]{3,1,0,2:T(8,128)} %get-tuple-element.385, ...), kind=kOutput, calls=%fused_computation.5.clone.1 | convolution fusion | flops 132464640 | bytes 2949133 | tf_op jit(solution)/shard_map/while/body/eval_jaxpr/iac,icub->iaub/dot_general | solution.py:36
  154.4 3.0 %convolution_add_fusion.5 = f32[6,64,7,64]{3,1,2,0:T(8,128)S(1)} fusion(f32[6,64,7,64]{3,1,2,0:T(8,128)S(1)} %get-tuple-element.372, f32[12,64,13,64]{3,1,2,0:T(8,128)} %get-tuple-element.386, s32[]{:T(128)S(6)} %select_n.77, s32[]{:T(128)S(6)} %select_n.79, pred[]{:T(512)S(6)} %compare.23, f32[6,64,7,64]{3,1,0,2:T(8,128)} %get-tuple-element.385, ...), kind=kOutput, calls=%fused_computation.5.clone.1 | convolution fusion | flops 132464640 | bytes 2949133 | tf_op jit(solution)/shard_map/while/body/eval_jaxpr/iac,icub->iaub/dot_general | solution.py:36
  162.6 3.0 %convolution_add_fusion.5 = f32[6,64,7,64]{3,1,2,0:T(8,128)S(1)} fusion(f32[6,64,7,64]{3,1,2,0:T(8,128)S(1)} %get-tuple-element.372, f32[12,64,13,64]{3,1,2,0:T(8,128)} %get-tuple-element.386, s32[]{:T(128)S(6)} %select_n.77, s32[]{:T(128)S(6)} %select_n.79, pred[]{:T(512)S(6)} %compare.23, f32[6,64,7,64]{3,1,0,2:T(8,128)} %get-tuple-element.385, ...), kind=kOutput, calls=%fused_computation.5.clone.1 | convolution fusion | flops 132464640 | bytes 2949133 | tf_op jit(solution)/shard_map/while/body/eval_jaxpr/iac,icub->iaub/dot_general | solution.py:36
  170.8 3.0 %convolution_add_fusion.5 = f32[6,64,7,64]{3,1,2,0:T(8,128)S(1)} fusion(f32[6,64,7,64]{3,1,2,0:T(8,128)S(1)} %get-tuple-element.372, f32[12,64,13,64]{3,1,2,0:T(8,128)} %get-tuple-element.386, s32[]{:T(128)S(6)} %select_n.77, s32[]{:T(128)S(6)} %select_n.79, pred[]{:T(512)S(6)} %compare.23, f32[6,64,7,64]{3,1,0,2:T(8,128)} %get-tuple-element.385, ...), kind=kOutput, calls=%fused_computation.5.clone.1 | convolution fusion | flops 132464640 | bytes 2949133 | tf_op jit(solution)/shard_map/while/body/eval_jaxpr/iac,icub->iaub/dot_general | solution.py:36
  (42 shorter events, 29.2 us)
Async XLA Ops:
  0.0 2.7 %copy-start.1 = (s32[6,7]{1,0:T(8,128)S(1)}, s32[6,7]{1,0:T(8,128)}, u32[]{:S(2)}) copy-start(s32[6,7]{1,0:T(8,128)} %param.8) | copy-start | bytes 508
  5.3 13.1 %collective-permute-start = (f32[3,64,7,64]{3,1,2,0:T(8,128)}, f32[3,64,7,64]{3,1,2,0:T(8,128)}, u32[]{:S(2)}, u32[]{:S(2)}) collective-permute-start(f32[3,64,7,64]{3,1,2,0:T(8,128)} %copy.11), channel_id=1, source_target_pairs={{0,1},{1,2},{2,3},{3,4},{4,5},{5,6},{6,7},{7,8},{8,9},{9,10},{10,1... | collective-permute-start | bytes 1032200 | tf_op jit(solution)/shard_map/ppermute | solution.py:18
  11.2 3.4 %copy-start.2 = (s32[6,7]{1,0:T(8,128)S(1)}, s32[6,7]{1,0:T(8,128)}, u32[]{:S(2)}) copy-start(s32[6,7]{1,0:T(8,128)} %param.9) | copy-start | bytes 508
  11.2 18.1 %collective-permute-start.1 = (f32[3,64,7,64]{3,1,2,0:T(8,128)}, f32[3,64,7,64]{3,1,2,0:T(8,128)}, u32[]{:S(2)}, u32[]{:S(2)}) collective-permute-start(f32[3,64,7,64]{3,1,2,0:T(8,128)} %copy.12), channel_id=1, source_target_pairs={{1,0},{2,1},{3,2},{4,3},{5,4},{6,5},{7,6},{8,7},{9,8},{10,9},{11,1... | collective-permute-start | bytes 1032200 | tf_op jit(solution)/shard_map/ppermute | solution.py:20
  93.2 10.1 %collective-permute-start.2 = (f32[3,64,7,64]{3,1,2,0:T(8,128)}, f32[3,64,7,64]{3,1,2,0:T(8,128)}, u32[]{:S(2)}, u32[]{:S(2)}) collective-permute-start(f32[3,64,7,64]{3,1,2,0:T(8,128)} %get-tuple-element.263), channel_id=1, source_target_pairs={{0,1},{1,2},{2,3},{3,4},{4,5},{5,6},{6,7},{7,8},{8,9},{9,10},{10,1... | collective-permute-start | bytes 1032200 | tf_op jit(solution)/shard_map/ppermute | solution.py:18
  95.1 17.8 %collective-permute-start.3 = (f32[3,64,7,64]{3,1,2,0:T(8,128)S(1)}, f32[3,64,7,64]{3,1,2,0:T(8,128)}, u32[]{:S(2)}, u32[]{:S(2)}) collective-permute-start(f32[3,64,7,64]{3,1,2,0:T(8,128)S(1)} %get-tuple-element.264), channel_id=1, source_target_pairs={{1,0},{2,1},{3,2},{4,3},{5,4},{6,5},{7,6},{8,7},{9,8},{10,9},{11,1... | collective-permute-start | bytes 1032200 | tf_op jit(solution)/shard_map/ppermute | solution.py:20
  116.6 57.3 %copy-start = (f32[6,64,7,64]{3,2,1,0:T(8,128)S(1)}, f32[6,64,7,64]{3,2,1,0:T(8,128)}, u32[]{:S(2)}) copy-start(f32[6,64,7,64]{3,2,1,0:T(8,128)} %reshape.8) | copy-start | bytes 2064388
where the time goes:
time: 180 us; the launch traced here: 179 us
  loops' own time  63.8 us (35%)
  matrix products  42.5 us (24%)
  waiting for transfers between devices  28.6 us (16%)
  local copies, waits for them, and re-layouts  24.3 us (14%)
  starting transfers between devices  11.2 us (6%)
  other arithmetic  7.97 us (4%)
    another operation x2, loops' own time, band_mult(): lax.scan(advance, zero_sum, jnp.arange(band_len, dtype=jnp.int32))  63.8 us
    dot_general x14, matrix products, advance(): jnp.einsum('iac,icub->iaub', left_block, window, precision=lax.Precision....  42.5 us
    ppermute x2, waiting for transfers between devices, with_halo(): lax.ppermute(head, axis, [((i + 1) % count, i) for i in range(count)])  19 us
    ppermute x2, waiting for transfers between devices, with_halo(): lax.ppermute(tail, axis, [(i, (i + 1) % count) for i in range(count)])  9.57 us
    dynamic_slice x14, local copies, waits for them, and re-layouts, band_mult(): lax.scan(advance, zero_sum, jnp.arange(band_len, dtype=jnp.int32))  8.2 us
    ppermute x2, starting transfers between devices, with_halo(): lax.ppermute(tail, axis, [(i, (i + 1) % count) for i in range(count)])  6.79 us
    ppermute x2, starting transfers between devices, with_halo(): lax.ppermute(head, axis, [((i + 1) % count, i) for i in range(count)])  4.45 us
    concatenate x2, other arithmetic, with_halo(): jnp.concatenate([lax.ppermute(tail, axis, [(i, (i + 1) % count) for i in...  4.09 us
  transfers between devices with their start and end apart: 4, of which 4 were waited for; matrix products, arithmetic and copies ran while one was open for 2% of the time, Pallas kernels for 0%

commit v1 on v0

v1 whole, which is shorter than its diff:
```python
import functools

import jax
import jax.numpy as jnp
from jax import lax
from jax.experimental import pallas as pl
from jax.experimental.pallas import tpu as pltpu
from jax.sharding import PartitionSpec as P

BS = 64
W = 7
ROWS = 6
MESH = pl.DeviceIdType.MESH
F32 = jnp.float32
BF16 = jnp.bfloat16


def split(value):
    high = value.astype(BF16)
    return high, (value - high.astype(F32)).astype(BF16)


def product(left, right):
    lhs = jnp.concatenate([left[0], left[0], left[1]], axis=1)
    rhs = jnp.concatenate([right[0], right[1], right[0]], axis=0)
    return jnp.dot(lhs, rhs, preferred_element_type=F32)


def kernel(
    x_hbm, xm_hbm, gm_hbm, z_hbm,
    x_v, xm_s, gm_s, xp, dh, dl, gh, gl, gacc, x_recv, p_send, p_recv, m_send, m_recv, z_v,
    in_sem, out_sem, send_sem, recv_sem,
):
    rows, cols = lax.axis_size("row"), lax.axis_size("col")
    flat = lax.axis_index("row") * cols + lax.axis_index("col")
    there = []
    for step in (rows * cols - 1, 1):
        other = lax.rem(flat + step, rows * cols)
        there.append((lax.div(other, cols), lax.rem(other, cols)))

    barrier = pltpu.get_barrier_semaphore()
    for device in there:
        pl.semaphore_signal(barrier, inc=1, device_id=device, device_id_type=MESH)

    loads = [pltpu.make_async_copy(xm_hbm, xm_s, in_sem.at[ROWS]), pltpu.make_async_copy(gm_hbm, gm_s, in_sem.at[ROWS + 1])]
    loads += [pltpu.make_async_copy(x_hbm.at[i], x_v.at[i], in_sem.at[i]) for i in range(ROWS)]
    for load in loads:
        load.start()
    for buffer in (dh, dl, gh, gl, m_send):
        buffer[...] = jnp.zeros_like(buffer)

    lane = lax.broadcasted_iota(jnp.int32, (1, 128), 1)
    low = lane < BS

    def window_mask(mask, i):
        def factor(t):
            return mask[i, t].astype(F32) if 0 <= t < W else jnp.float32(0)

        first = -(i % 2)
        return jnp.concatenate(
            [jnp.where(low, factor(first + 2 * u), factor(first + 2 * u + 1)) for u in range(4)], axis=1
        )

    loads[0].wait()
    loads[1].wait()
    blank = jnp.zeros((BS, BS), F32)
    for i in range(ROWS):
        loads[2 + i].wait()
        value = x_v[i]
        value = jnp.concatenate([value, blank] if i % 2 == 0 else [blank, value], axis=1) * window_mask(xm_s, i)
        xp[i] = value
        high, rest = split(value)
        span = slice(192 + 64 * i, 256 + 64 * i), slice(128 * (i // 2), 128 * (i // 2) + 512)
        dh[span] = high
        dl[span] = rest
    for i in range(3):
        ours = window_mask(gm_s, i)
        m_send[0, i : i + 1, 128 * (i // 2) : 384] = ours[:, : 384 - 128 * (i // 2)]
        ours = window_mask(gm_s, 3 + i)
        start = 384 - 128 * ((3 + i) // 2)
        m_send[1, i : i + 1, 0 : 512 - start] = ours[:, start:]

    pl.semaphore_wait(barrier, 2)

    pieces = [
        [
            (xp.at[0:2, :, 0:384], x_recv.at[1, 0:2]),
            (xp.at[2, :, 0:256], x_recv.at[1, 2, :, 128:384]),
            (m_send.at[0], m_recv.at[1]),
            (p_send.at[0], p_recv.at[1]),
        ],
        [
            (xp.at[4:6, :, 128:512], x_recv.at[0, 1:3]),
            (xp.at[3, :, 256:512], x_recv.at[0, 0, :, 0:256]),
            (m_send.at[1], m_recv.at[0]),
            (p_send.at[1], p_recv.at[0]),
        ],
    ]

    def remote(side, number, from_side):
        src, dst = pieces[side][number]
        return pltpu.make_async_remote_copy(
            src_ref=src, dst_ref=dst, send_sem=send_sem.at[side, number], recv_sem=recv_sem.at[from_side, number],
            device_id=there[side], device_id_type=MESH,
        )

    sends = [[remote(side, number, 1 - side) for number in range(4)] for side in (0, 1)]

    def arrived(side, number):
        remote(1 - side, number, side).wait_recv()

    for number in (0, 1, 2):
        for side in (0, 1):
            sends[side][number].start()

    def d(row, height, column, width):
        span = slice(row, row + height), slice(column, column + width)
        return dh[span], dl[span]

    to_left = product(d(192, 192, 384, 256), d(384, 256, 128, 256))
    to_right = product(d(384, 192, 128, 256), d(128, 256, 384, 256))
    for side, whole, half in ((0, to_left[:, 128:], to_left[:, :128]), (1, to_right[:, :128], to_right[:, 128:])):
        p_send[side, 0:192] = whole
        p_send[side, 192:288] = half[0:96] + pltpu.roll(half[96:192], 64, 1)
        sends[side][3].start()

    for p in range(3):
        gacc[p] = product(d(192 + 128 * p, 128, 256, 256), d(256, 256, 128 * p, 512))

    def put_g(row, column, value):
        high, rest = split(value)
        span = slice(row, row + value.shape[0]), slice(column, column + value.shape[1])
        gh[span] = high
        gl[span] = rest

    def put_pair(p, value):
        for i in (2 * p, 2 * p + 1):
            put_g(192 + 64 * i, 128 * p, value[64 * (i % 2) : 64 * (i % 2) + 64] * window_mask(gm_s, i))

    for side in (0, 1):
        arrived(side, 0)
        arrived(side, 1)
        for r in range(3):
            row = 64 * r + 576 * side
            short = (r == 0) if side == 0 else (r == 2)
            if side == 0:
                value, column = (x_recv[0, r, :, 0:256] if short else x_recv[0, r]), 0
            else:
                value, column = (x_recv[1, r, :, 128:384], 512) if short else (x_recv[1, r], 384)
            high, rest = split(value)
            span = slice(row, row + 64), slice(column, column + value.shape[1])
            dh[span] = high
            dl[span] = rest
        if side == 0:
            outer = product(d(0, 448, 0, 256), d(0, 256, 0, 512))
            halo = outer[0:192, 0:384] + product(d(0, 192, 256, 256), d(256, 256, 0, 384))
            put_pair(0, gacc[0] + outer[192:320])
            gacc[1, :, 0:384] += outer[320:448, 128:512]
        else:
            outer = product(d(320, 448, 512, 256), d(512, 256, 256, 512))
            halo = outer[256:448, 128:512] + product(d(576, 192, 256, 256), d(256, 256, 384, 384))
            put_pair(2, gacc[2] + outer[128:256])
            gacc[1, :, 128:512] += outer[0:128, 0:384]
            put_pair(1, gacc[1])
        arrived(side, 2)
        arrived(side, 3)
        whole = p_recv[side, 0:192]
        half = p_recv[side, 192:288]
        half = jnp.concatenate([half, pltpu.roll(half, 64, 1)], axis=0)
        if side == 0:
            extra = [whole, jnp.where(low, half, 0.0), jnp.zeros((192, 128), F32)]
        else:
            extra = [jnp.zeros((192, 128), F32), jnp.where(low, 0.0, half), whole]
        halo = halo + jnp.concatenate(extra, axis=1)
        for r in range(3):
            put_g(64 * r + 576 * side, 384 * side, halo[64 * r : 64 * r + 64] * m_recv[side, r : r + 1])

    def g(row, height, column, width):
        span = slice(row, row + height), slice(column, column + width)
        return gh[span], gl[span]

    stores = []
    for p in range(3):
        cubic = product(d(192 + 128 * p, 128, 128 * p, 512), g(128 * p, 512, 128 * p, 512))
        for i in (2 * p, 2 * p + 1):
            start = 64 * (i % 2)
            z = 1.5 * xp[i] - (0.5 * window_mask(xm_s, i)) * cubic[start : start + 64]
            z_v[i] = z[:, start : start + W * BS]
            stores.append(pltpu.make_async_copy(z_v.at[i], z_hbm.at[i], out_sem.at[i]))
            stores[-1].start()

    for side in (0, 1):
        for copy in sends[side]:
            copy.wait_send()
    for store in stores:
        store.wait()


def body(x_band, x_mask, g_mask):
    return pl.pallas_call(
        kernel,
        out_shape=jax.ShapeDtypeStruct(x_band.shape, F32),
        in_specs=[pl.BlockSpec(memory_space=pl.ANY)] * 3,
        out_specs=pl.BlockSpec(memory_space=pl.ANY),
        scratch_shapes=[
            pltpu.VMEM((ROWS, BS, W * BS), F32),
            pltpu.SMEM((ROWS, W), jnp.int32),
            pltpu.SMEM((ROWS, W), jnp.int32),
            pltpu.VMEM((ROWS, BS, 512), F32),
            pltpu.VMEM((768, 768), BF16),
            pltpu.VMEM((768, 768), BF16),
            pltpu.VMEM((768, 768), BF16),
            pltpu.VMEM((768, 768), BF16),
            pltpu.VMEM((3, 128, 512), F32),
            pltpu.VMEM((2, 3, BS, 384), F32),
            pltpu.VMEM((2, 288, 128), F32),
            pltpu.VMEM((2, 288, 128), F32),
            pltpu.VMEM((2, 8, 384), F32),
            pltpu.VMEM((2, 8, 384), F32),
            pltpu.VMEM((ROWS, BS, W * BS), F32),
            pltpu.SemaphoreType.DMA((ROWS + 2,)),
            pltpu.SemaphoreType.DMA((ROWS,)),
            pltpu.SemaphoreType.DMA((2, 4)),
            pltpu.SemaphoreType.DMA((2, 4)),
        ],
        compiler_params=pltpu.CompilerParams(
            collective_id=0, has_side_effects=True, vmem_limit_bytes=48 * 1024 * 1024
        ),
        cost_estimate=pl.CostEstimate(flops=1_000_000_000, bytes_accessed=1_500_000, transcendentals=0),
    )(x_band, x_mask, g_mask)


def solution(mesh):
    placed = (P(("row", "col"), None, None), P(("row", "col"), None), P(("row", "col"), None))
    return jax.shard_map(
        body, mesh=mesh, in_specs=placed, out_specs=P(("row", "col"), None, None), check_vma=False
    )
```

time: 180 us -> 28.4 us (0.16)
  the two profiles are of different devices: /device:TPU:255 before, /device:TPU:1 now
where the time goes in v1:
time: 28.4 us; the launch traced here: 28.1 us
  Pallas kernels  24.7 us (87%)
  local copies, waits for them, and re-layouts  3.39 us (12%)
    pallas_call x1, Pallas kernels, body(): pl.pallas_call(kernel, out_shape=jax.ShapeDtypeStruct(x_band.shape, F32),...  24.7 us
    unnamed x7, local copies, waits for them, and re-layouts  3.39 us

profile of v1, /device:TPU:1, one launch (start us, length us, event | category | flops | bytes accessed | tf_op | source)
XLA Modules:
  0.0 28.1 jit_solution(9136158032405828624)
XLA Ops:
  0.0 0.0 copy-start
  0.0 1.1 %copy-done = f32[6,64,448]{2,1,0:T(8,128)S(1)} copy-done((f32[6,64,448]{2,1,0:T(8,128)S(1)}, f32[6,64,448]{2,1,0:T(8,128)}, u32[]{:S(2)}) %copy-start) | copy-done | bytes 688152
  1.1 0.0 copy-start.1
  1.1 0.7 %copy-done.1 = s32[6,7]{1,0:T(8,128)S(1)} copy-done((s32[6,7]{1,0:T(8,128)S(1)}, s32[6,7]{1,0:T(8,128)}, u32[]{:S(2)}) %copy-start.1) | copy-done | bytes 192
  1.8 0.0 copy-start.2
  1.8 0.7 %copy-done.2 = s32[6,7]{1,0:T(8,128)S(1)} copy-done((s32[6,7]{1,0:T(8,128)S(1)}, s32[6,7]{1,0:T(8,128)}, u32[]{:S(2)}) %copy-start.2) | copy-done | bytes 192
  2.5 24.7 %shard_map.37 = f32[6,64,448]{2,1,0:T(8,128)S(1)} custom-call(f32[6,64,448]{2,1,0:T(8,128)S(1)} %copy-done, s32[6,7]{1,0:T(8,128)S(1)} %copy-done.1, s32[6,7]{1,0:T(8,128)S(1)} %copy-done.2), custom_call_target="tpu_custom_call" | custom-call | flops 1000000000 | bytes 1500000 | tf_op jit(solution)/shard_map/pallas_call | solution.py:200
  27.2 0.9 %copy.5 = f32[6,64,448]{2,1,0:T(8,128)} copy(f32[6,64,448]{2,1,0:T(8,128)S(1)} %shard_map.37) | data formatting | bytes 1376256
Async XLA Ops:
  0.0 1.1 %copy-start = (f32[6,64,448]{2,1,0:T(8,128)S(1)}, f32[6,64,448]{2,1,0:T(8,128)}, u32[]{:S(2)}) copy-start(f32[6,64,448]{2,1,0:T(8,128)} %x_hbm.1) | copy-start | bytes 2064388
  1.1 0.7 %copy-start.1 = (s32[6,7]{1,0:T(8,128)S(1)}, s32[6,7]{1,0:T(8,128)}, u32[]{:S(2)}) copy-start(s32[6,7]{1,0:T(8,128)} %xm_hbm.1) | copy-start | bytes 508
  1.8 0.7 %copy-start.2 = (s32[6,7]{1,0:T(8,128)S(1)}, s32[6,7]{1,0:T(8,128)}, u32[]{:S(2)}) copy-start(s32[6,7]{1,0:T(8,128)} %gm_hbm.1) | copy-start | bytes 508

commit v2 on v1

v2 whole, which is shorter than its diff:
```python
import functools

import jax
import jax.numpy as jnp
from jax import lax
from jax.experimental import pallas as pl
from jax.experimental.pallas import tpu as pltpu
from jax.sharding import PartitionSpec as P

BS = 64
W = 7
ROWS = 6
MESH = pl.DeviceIdType.MESH
F32 = jnp.float32
BF16 = jnp.bfloat16


def split(value):
    high = value.astype(BF16)
    return high, (value - high.astype(F32)).astype(BF16)


def product(left, right):
    lhs = jnp.concatenate([left[0], left[0], left[1]], axis=1)
    rhs = jnp.concatenate([right[0], right[1], right[0]], axis=0)
    return jnp.dot(lhs, rhs, preferred_element_type=F32)


def kernel(
    x_hbm, xm_hbm, gm_hbm, z_out,
    x_v, xm_s, gm_s, xp, dh, dl, gh, gl, gacc, x_recv, p_send, p_recv, m_send, m_recv,
    zacc, in_sem, send_sem, recv_sem, left_here,
):
    rows, cols = lax.axis_size("row"), lax.axis_size("col")
    flat = lax.axis_index("row") * cols + lax.axis_index("col")
    there = []
    for step in (rows * cols - 1, 1):
        other = lax.rem(flat + step, rows * cols)
        there.append((lax.div(other, cols), lax.rem(other, cols)))

    barrier = pltpu.get_barrier_semaphore()
    pl.semaphore_signal(barrier, inc=1, device_id=there[0], device_id_type=MESH)

    order = (3, 4, 5, 0, 1, 2)
    loads = [pltpu.make_async_copy(x_hbm.at[i], x_v.at[i], in_sem.at[i]) for i in range(ROWS)]
    mask_loads = [pltpu.make_async_copy(xm_hbm, xm_s, in_sem.at[ROWS]), pltpu.make_async_copy(gm_hbm, gm_s, in_sem.at[ROWS + 1])]
    for load in mask_loads:
        load.start()
    for i in order:
        loads[i].start()
    for buffer in (dh, dl, m_send):
        buffer[...] = jnp.zeros_like(buffer)

    lane = lax.broadcasted_iota(jnp.int32, (1, 128), 1)
    low = lane < BS

    def window_mask(mask, i):
        def factor(t):
            return mask[i, t].astype(F32) if 0 <= t < W else jnp.float32(0)

        first = -(i % 2)
        return jnp.concatenate(
            [jnp.where(low, factor(first + 2 * u), factor(first + 2 * u + 1)) for u in range(4)], axis=1
        )

    pieces = [
        [
            (xp.at[0:2, :, 0:384], x_recv.at[1, 0:2]),
            (xp.at[2, :, 0:256], x_recv.at[1, 2, :, 128:384]),
            (m_send.at[0], m_recv.at[1]),
            (p_send.at[0], p_recv.at[1]),
        ],
        [
            (xp.at[4:6, :, 128:512], x_recv.at[0, 1:3]),
            (xp.at[3, :, 256:512], x_recv.at[0, 0, :, 0:256]),
            (m_send.at[1], m_recv.at[0]),
            (p_send.at[1], p_recv.at[0]),
        ],
    ]

    def remote(side, number, from_side):
        src, dst = pieces[side][number]
        return pltpu.make_async_remote_copy(
            src_ref=src, dst_ref=dst, send_sem=send_sem.at[side, number], recv_sem=recv_sem.at[from_side, number],
            device_id=there[side], device_id_type=MESH,
        )

    sends = [[remote(side, number, 1 - side) for number in range(4)] for side in (0, 1)]

    def arrived(side, number):
        remote(1 - side, number, side).wait_recv()

    blank = jnp.zeros((BS, BS), F32)

    def prepare(i):
        loads[i].wait()
        value = x_v[i]
        value = jnp.concatenate([value, blank] if i % 2 == 0 else [blank, value], axis=1) * window_mask(xm_s, i)
        xp[i] = value
        high, rest = split(value)
        span = slice(192 + 64 * i, 256 + 64 * i), slice(128 * (i // 2), 128 * (i // 2) + 512)
        dh[span] = high
        dl[span] = rest

    def d(row, height, column, width):
        span = slice(row, row + height), slice(column, column + width)
        return dh[span], dl[span]

    def g(row, height, column, width):
        span = slice(row, row + height), slice(column, column + width)
        return gh[span], gl[span]

    for load in mask_loads:
        load.wait()
    for i in (3, 4, 5):
        prepare(i)
        start = 384 - 128 * (i // 2)
        m_send[1, i - 3 : i - 2, 0 : 512 - start] = window_mask(gm_s, i)[:, start:]
    pl.semaphore_wait(barrier, 1)
    pl.semaphore_signal(left_here, inc=1, device_id=there[1], device_id_type=MESH)
    for number in (0, 1, 2):
        sends[1][number].start()
    for i in (0, 1, 2):
        prepare(i)
        m_send[0, i : i + 1, 128 * (i // 2) : 384] = window_mask(gm_s, i)[:, : 384 - 128 * (i // 2)]

    to_right = product(d(384, 192, 128, 256), d(128, 256, 384, 256))
    p_send[1, 0:192] = to_right[:, :128]
    p_send[1, 192:288] = to_right[0:96, 128:] + pltpu.roll(to_right[96:192, 128:], 64, 1)
    sends[1][3].start()
    to_left = product(d(192, 192, 384, 256), d(384, 256, 128, 256))
    p_send[0, 0:192] = to_left[:, 128:]
    p_send[0, 192:288] = to_left[0:96, :128] + pltpu.roll(to_left[96:192, :128], 64, 1)

    pl.semaphore_wait(left_here, 1)
    for number in range(4):
        sends[0][number].start()

    for buffer in (gh, gl):
        buffer[...] = jnp.zeros_like(buffer)
    for p in range(3):
        gacc[p] = product(d(192 + 128 * p, 128, 256, 256), d(256, 256, 128 * p, 512))

    def put_g(row, column, value):
        high, rest = split(value)
        span = slice(row, row + value.shape[0]), slice(column, column + value.shape[1])
        gh[span] = high
        gl[span] = rest

    def put_pair(p, value):
        for i in (2 * p, 2 * p + 1):
            put_g(192 + 64 * i, 128 * p, value[64 * (i % 2) : 64 * (i % 2) + 64] * window_mask(gm_s, i))

    def take_x(side):
        arrived(side, 0)
        arrived(side, 1)
        for r in range(3):
            short = (r == 0) if side == 0 else (r == 2)
            if side == 0:
                value, column = (x_recv[0, r, :, 0:256] if short else x_recv[0, r]), 0
            else:
                value, column = (x_recv[1, r, :, 128:384], 512) if short else (x_recv[1, r], 384)
            high, rest = split(value)
            span = slice(64 * r + 576 * side, 64 * r + 576 * side + 64), slice(column, column + value.shape[1])
            dh[span] = high
            dl[span] = rest

    def take_p(side, halo):
        arrived(side, 2)
        arrived(side, 3)
        whole = p_recv[side, 0:192]
        half = p_recv[side, 192:288]
        half = jnp.concatenate([half, pltpu.roll(half, 64, 1)], axis=0)
        if side == 0:
            sums = [halo[:, 0:128] + whole, halo[:, 128:256] + jnp.where(low, half, 0.0), halo[:, 256:384]]
        else:
            sums = [halo[:, 0:128], halo[:, 128:256] + jnp.where(low, 0.0, half), halo[:, 256:384] + whole]
        halo = jnp.concatenate(sums, axis=1)
        for r in range(3):
            put_g(64 * r + 576 * side, 384 * side, halo[64 * r : 64 * r + 64] * m_recv[side, r : r + 1])

    def finish(p, cubic):
        for i in (2 * p, 2 * p + 1):
            start = 64 * (i % 2)
            z = 1.5 * xp[i] - (0.5 * window_mask(xm_s, i)) * cubic[start : start + 64]
            z_out[i] = z[:, start : start + W * BS]

    take_x(1)
    outer = product(d(320, 448, 512, 256), d(512, 256, 256, 512))
    halo = outer[256:448, 128:512] + product(d(576, 192, 256, 256), d(256, 256, 384, 384))
    gacc[1, :, 128:512] += outer[0:128, 0:384]
    put_pair(2, gacc[2] + outer[128:256])
    take_p(1, halo)
    cubic = product(d(320, 256, 512, 256), g(512, 256, 256, 512))
    zacc[1, :, 0:128] = jnp.zeros((128, 128), F32)
    zacc[1, :, 128:512] = cubic[0:128, 0:384]
    zacc[2] = cubic[128:256]

    take_x(0)
    outer = product(d(0, 448, 0, 256), d(0, 256, 0, 512))
    put_pair(0, gacc[0] + outer[192:320])
    gacc[1, :, 0:384] += outer[320:448, 128:512]
    put_pair(1, gacc[1])
    halo = outer[0:192, 0:384] + product(d(0, 192, 256, 256), d(256, 256, 0, 384))
    zacc[0] = product(d(192, 128, 256, 256), g(256, 256, 0, 512))
    zacc[1] += product(d(320, 128, 256, 256), g(256, 256, 128, 512))
    finish(2, zacc[2] + product(d(448, 128, 256, 256), g(256, 256, 256, 512)))
    take_p(0, halo)
    cubic = product(d(192, 256, 0, 256), g(0, 256, 0, 512))
    finish(0, zacc[0] + cubic[0:128])
    zacc[1, :, 0:384] += cubic[128:256, 128:512]
    finish(1, zacc[1])

    for side in (0, 1):
        for copy in sends[side]:
            copy.wait_send()


def body(x_band, x_mask, g_mask):
    return pl.pallas_call(
        kernel,
        out_shape=jax.ShapeDtypeStruct(x_band.shape, F32),
        in_specs=[pl.BlockSpec(memory_space=pltpu.HBM)] * 3,
        out_specs=pl.BlockSpec(memory_space=pltpu.VMEM),
        scratch_shapes=[
            pltpu.VMEM((ROWS, BS, W * BS), F32),
            pltpu.SMEM((ROWS, W), jnp.int32),
            pltpu.SMEM((ROWS, W), jnp.int32),
            pltpu.VMEM((ROWS, BS, 512), F32),
            pltpu.VMEM((768, 768), BF16),
            pltpu.VMEM((768, 768), BF16),
            pltpu.VMEM((768, 768), BF16),
            pltpu.VMEM((768, 768), BF16),
            pltpu.VMEM((3, 128, 512), F32),
            pltpu.VMEM((2, 3, BS, 384), F32),
            pltpu.VMEM((2, 288, 128), F32),
            pltpu.VMEM((2, 288, 128), F32),
            pltpu.VMEM((2, 8, 384), F32),
            pltpu.VMEM((2, 8, 384), F32),
            pltpu.VMEM((3, 128, 512), F32),
            pltpu.SemaphoreType.DMA((ROWS + 2,)),
            pltpu.SemaphoreType.DMA((2, 4)),
            pltpu.SemaphoreType.DMA((2, 4)),
            pltpu.SemaphoreType.REGULAR,
        ],
        compiler_params=pltpu.CompilerParams(
            collective_id=0, has_side_effects=True, vmem_limit_bytes=48 * 1024 * 1024
        ),
        cost_estimate=pl.CostEstimate(flops=1_000_000_000, bytes_accessed=1_500_000, transcendentals=0),
    )(*(pltpu.with_memory_space_constraint(a, pltpu.HBM) for a in (x_band, x_mask, g_mask)))


def solution(mesh):
    placed = (P(("row", "col"), None, None), P(("row", "col"), None), P(("row", "col"), None))
    return jax.shard_map(
        body, mesh=mesh, in_specs=placed, out_specs=P(("row", "col"), None, None), check_vma=False
    )
```

time: 28.4 us -> 19.9 us (0.70)
  the two profiles are of different devices: /device:TPU:1 before, /device:TPU:255 now
where the time goes in v2:
time: 19.9 us; the launch traced here: 19.8 us
  Pallas kernels  18.9 us (95%)
  local copies, waits for them, and re-layouts  0.88 us (4%)
    pallas_call x1, Pallas kernels, body(): pl.pallas_call(kernel, out_shape=jax.ShapeDtypeStruct(x_band.shape, F32),...  18.9 us
    unnamed x1, local copies, waits for them, and re-layouts  0.88 us

profile of v2, /device:TPU:255, one launch (start us, length us, event | category | flops | bytes accessed | tf_op | source)
XLA Modules:
  0.0 19.8 jit_solution(7471395751136616880)
XLA Ops:
  0.0 18.9 %shard_map.37 = f32[6,64,448]{2,1,0:T(8,128)S(1)} custom-call(f32[6,64,448]{2,1,0:T(8,128)} %x_hbm.1, s32[6,7]{1,0:T(8,128)} %xm_hbm.1, s32[6,7]{1,0:T(8,128)} %gm_hbm.1), custom_call_target="tpu_custom_call" | custom-call | flops 1000000000 | bytes 1500000 | tf_op jit(solution)/shard_map/pallas_call | solution.py:220
  18.9 0.9 %copy.5 = f32[6,64,448]{2,1,0:T(8,128)} copy(f32[6,64,448]{2,1,0:T(8,128)S(1)} %shard_map.37) | data formatting | bytes 1376256

commit v3 on v2

--- a/solution.py
+++ b/solution.py
@@ -38,8 +38,14 @@
         other = lax.rem(flat + step, rows * cols)
         there.append((lax.div(other, cols), lax.rem(other, cols)))
 
+    first_two = flat < 2
     barrier = pltpu.get_barrier_semaphore()
     pl.semaphore_signal(barrier, inc=1, device_id=there[0], device_id_type=MESH)
+    replies = jnp.logical_or(flat == 0, flat == rows * cols - 1)
+
+    @pl.when(jnp.logical_not(replies))
+    def _():
+        pl.semaphore_signal(barrier, inc=1, device_id=there[1], device_id_type=MESH)
 
     order = (3, 4, 5, 0, 1, 2)
     loads = [pltpu.make_async_copy(x_hbm.at[i], x_v.at[i], in_sem.at[i]) for i in range(ROWS)]
@@ -50,6 +56,11 @@
         loads[i].start()
     for buffer in (dh, dl, m_send):
         buffer[...] = jnp.zeros_like(buffer)
+
+    @pl.when(replies)
+    def _():
+        pl.semaphore_wait(barrier, jnp.where(flat == 0, 1, 2))
+        pl.semaphore_signal(left_here, inc=1, device_id=there[1], device_id_type=MESH)
 
     lane = lax.broadcasted_iota(jnp.int32, (1, 128), 1)
     low = lane < BS
@@ -116,13 +127,21 @@
         prepare(i)
         start = 384 - 128 * (i // 2)
         m_send[1, i - 3 : i - 2, 0 : 512 - start] = window_mask(gm_s, i)[:, start:]
-    pl.semaphore_wait(barrier, 1)
-    pl.semaphore_signal(left_here, inc=1, device_id=there[1], device_id_type=MESH)
+
+    @pl.when(jnp.logical_not(replies))
+    def _():
+        pl.semaphore_wait(barrier, jnp.where(flat == 1, 1, 2))
+
     for number in (0, 1, 2):
         sends[1][number].start()
     for i in (0, 1, 2):
         prepare(i)
         m_send[0, i : i + 1, 128 * (i // 2) : 384] = window_mask(gm_s, i)[:, : 384 - 128 * (i // 2)]
+
+    @pl.when(jnp.logical_not(first_two))
+    def _():
+        for number in (0, 1, 2):
+            sends[0][number].start()
 
     to_right = product(d(384, 192, 128, 256), d(128, 256, 384, 256))
     p_send[1, 0:192] = to_right[:, :128]
@@ -132,9 +151,9 @@
     p_send[0, 0:192] = to_left[:, 128:]
     p_send[0, 192:288] = to_left[0:96, :128] + pltpu.roll(to_left[96:192, :128], 64, 1)
 
-    pl.semaphore_wait(left_here, 1)
-    for number in range(4):
-        sends[0][number].start()
+    @pl.when(jnp.logical_not(first_two))
+    def _():
+        sends[0][3].start()
 
     for buffer in (gh, gl):
         buffer[...] = jnp.zeros_like(buffer)
@@ -185,31 +204,70 @@
             z = 1.5 * xp[i] - (0.5 * window_mask(xm_s, i)) * cubic[start : start + 64]
             z_out[i] = z[:, start : start + W * BS]
 
-    take_x(1)
-    outer = product(d(320, 448, 512, 256), d(512, 256, 256, 512))
-    halo = outer[256:448, 128:512] + product(d(576, 192, 256, 256), d(256, 256, 384, 384))
-    gacc[1, :, 128:512] += outer[0:128, 0:384]
-    put_pair(2, gacc[2] + outer[128:256])
-    take_p(1, halo)
-    cubic = product(d(320, 256, 512, 256), g(512, 256, 256, 512))
-    zacc[1, :, 0:128] = jnp.zeros((128, 128), F32)
-    zacc[1, :, 128:512] = cubic[0:128, 0:384]
-    zacc[2] = cubic[128:256]
-
-    take_x(0)
-    outer = product(d(0, 448, 0, 256), d(0, 256, 0, 512))
-    put_pair(0, gacc[0] + outer[192:320])
-    gacc[1, :, 0:384] += outer[320:448, 128:512]
-    put_pair(1, gacc[1])
-    halo = outer[0:192, 0:384] + product(d(0, 192, 256, 256), d(256, 256, 0, 384))
-    zacc[0] = product(d(192, 128, 256, 256), g(256, 256, 0, 512))
-    zacc[1] += product(d(320, 128, 256, 256), g(256, 256, 128, 512))
-    finish(2, zacc[2] + product(d(448, 128, 256, 256), g(256, 256, 256, 512)))
-    take_p(0, halo)
-    cubic = product(d(192, 256, 0, 256), g(0, 256, 0, 512))
-    finish(0, zacc[0] + cubic[0:128])
-    zacc[1, :, 0:384] += cubic[128:256, 128:512]
-    finish(1, zacc[1])
+    def over(side):
+        take_x(side)
+        if side == 0:
+            outer = product(d(0, 448, 0, 256), d(0, 256, 0, 512))
+            return outer[192:320], outer[320:448, 128:512], outer[0:192, 0:384]
+        outer = product(d(320, 448, 512, 256), d(512, 256, 256, 512))
+        return outer[128:256], outer[0:128, 0:384], outer[256:448, 128:512]
+
+    def halo_over(side):
+        if side == 0:
+            return product(d(0, 192, 256, 256), d(256, 256, 0, 384))
+        return product(d(576, 192, 256, 256), d(256, 256, 384, 384))
+
+    def cubic_over(side):
+        if side == 0:
+            cubic = product(d(192, 256, 0, 256), g(0, 256, 0, 512))
+            return cubic[0:128], cubic[128:256, 128:512]
+        cubic = product(d(320, 256, 512, 256), g(512, 256, 256, 512))
+        return cubic[128:256], cubic[0:128, 0:384]
+
+    def cubic_within(p):
+        return product(d(192 + 128 * p, 128, 256, 256), g(256, 256, 128 * p, 512))
+
+    def both_sides(first):
+        last = 1 - first
+        near, far = (slice(0, 384), slice(128, 512)) if first == 0 else (slice(128, 512), slice(0, 384))
+        edge, middle, halo = over(first)
+        gacc[1, :, near] += middle
+        put_pair(2 * first, gacc[2 * first] + edge)
+        take_p(first, halo + halo_over(first))
+        edge, middle = cubic_over(first)
+        zacc[2 * first] = edge
+        zacc[1] = jnp.zeros((128, 512), F32)
+        zacc[1, :, near] = middle
+
+        @pl.when(first_two)
+        def _():
+            pl.semaphore_wait(left_here, 1)
+            for number in range(4):
+                sends[0][number].start()
+
+        edge, middle, halo = over(last)
+        put_pair(2 * last, gacc[2 * last] + edge)
+        gacc[1, :, far] += middle
+        put_pair(1, gacc[1])
+        halo += halo_over(last)
+        finish(2 * first, zacc[2 * first] + cubic_within(2 * first))
+        zacc[2 * last] = cubic_within(2 * last)
+        zacc[1] += cubic_within(1)
+        take_p(last, halo)
+        edge, middle = cubic_over(last)
+        finish(2 * last, zacc[2 * last] + edge)
+        zacc[1, :, far] += middle
+        finish(1, zacc[1])
+
+    right_last = jnp.logical_and(lax.rem(flat, 2) == 1, flat != 1)
+
+    @pl.when(jnp.logical_not(right_last))
+    def _():
+        both_sides(1)
+
+    @pl.when(right_last)
+    def _():
+        both_sides(0)
 
     for side in (0, 1):
         for copy in sends[side]:

time: 19.9 us -> 17.6 us (0.88)
  the two profiles are of different devices: /device:TPU:255 before, /device:TPU:0 now
where the time goes in v3:
time: 17.6 us; the launch traced here: 17.5 us
  Pallas kernels  16.6 us (94%)
  local copies, waits for them, and re-layouts  0.88 us (5%)
    pallas_call x1, Pallas kernels, body(): pl.pallas_call(kernel, out_shape=jax.ShapeDtypeStruct(x_band.shape, F32),...  16.6 us
    unnamed x1, local copies, waits for them, and re-layouts  0.88 us

profile of v3, /device:TPU:0, one launch (start us, length us, event | category | flops | bytes accessed | tf_op | source)
XLA Modules:
  0.0 17.5 jit_solution(17507572834578284858)
XLA Ops:
  0.0 16.6 %shard_map.37 = f32[6,64,448]{2,1,0:T(8,128)S(1)} custom-call(f32[6,64,448]{2,1,0:T(8,128)} %x_hbm.1, s32[6,7]{1,0:T(8,128)} %xm_hbm.1, s32[6,7]{1,0:T(8,128)} %gm_hbm.1), custom_call_target="tpu_custom_call" | custom-call | flops 1000000000 | bytes 1500000 | tf_op jit(solution)/shard_map/pallas_call | solution.py:278
  16.6 0.9 %copy.5 = f32[6,64,448]{2,1,0:T(8,128)} copy(f32[6,64,448]{2,1,0:T(8,128)S(1)} %shard_map.37) | data formatting | bytes 1376256

commit v4 on v3

--- a/solution.py
+++ b/solution.py
@@ -47,14 +47,13 @@
     def _():
         pl.semaphore_signal(barrier, inc=1, device_id=there[1], device_id_type=MESH)
 
-    order = (3, 4, 5, 0, 1, 2)
     loads = [pltpu.make_async_copy(x_hbm.at[i], x_v.at[i], in_sem.at[i]) for i in range(ROWS)]
     mask_loads = [pltpu.make_async_copy(xm_hbm, xm_s, in_sem.at[ROWS]), pltpu.make_async_copy(gm_hbm, gm_s, in_sem.at[ROWS + 1])]
     for load in mask_loads:
         load.start()
-    for i in order:
+    for i in (3, 4, 5, 0, 1, 2):
         loads[i].start()
-    for buffer in (dh, dl, m_send):
+    for buffer in (dh, dl):
         buffer[...] = jnp.zeros_like(buffer)
 
     @pl.when(replies)
@@ -76,13 +75,15 @@
 
     pieces = [
         [
-            (xp.at[0:2, :, 0:384], x_recv.at[1, 0:2]),
+            (xp.at[0, :, 0:384], x_recv.at[1, 0]),
+            (xp.at[1, :, 128:384], x_recv.at[1, 1, :, 128:384]),
             (xp.at[2, :, 0:256], x_recv.at[1, 2, :, 128:384]),
             (m_send.at[0], m_recv.at[1]),
             (p_send.at[0], p_recv.at[1]),
         ],
         [
-            (xp.at[4:6, :, 128:512], x_recv.at[0, 1:3]),
+            (xp.at[5, :, 128:512], x_recv.at[0, 2]),
+            (xp.at[4, :, 128:384], x_recv.at[0, 1, :, 0:256]),
             (xp.at[3, :, 256:512], x_recv.at[0, 0, :, 0:256]),
             (m_send.at[1], m_recv.at[0]),
             (p_send.at[1], p_recv.at[0]),
@@ -96,7 +97,7 @@
             device_id=there[side], device_id_type=MESH,
         )
 
-    sends = [[remote(side, number, 1 - side) for number in range(4)] for side in (0, 1)]
+    sends = [[remote(side, number, 1 - side) for number in range(5)] for side in (0, 1)]
 
     def arrived(side, number):
         remote(1 - side, number, side).wait_recv()
@@ -113,6 +114,26 @@
         dh[span] = high
         dl[span] = rest
 
+    def pattern_row(side, r, t):
+        skipped = (0, 2) if side == 0 else (2, 0)
+        return None if (r, t) == skipped else 32 + 3 * r + t - (3 * r + t > 3 * skipped[0] + skipped[1])
+
+    def put_pattern(side, i):
+        ours = window_mask(gm_s, i)
+        for t in range(3):
+            row = pattern_row(1 - side, i % 3, t)
+            start = 128 * (t + 3 * side - i // 2)
+            if row is not None:
+                m_send[side, row : row + 1] = ours[:, start : start + 128]
+
+    def pack(value):
+        half = value.shape[0] // 2
+        return value[:half] + pltpu.roll(value[half:], 64, 1)
+
+    def unpack(value, side):
+        value = jnp.concatenate([value, pltpu.roll(value, 64, 1)], axis=0)
+        return jnp.where(low, value, 0.0) if side == 0 else jnp.where(low, 0.0, value)
+
     def d(row, height, column, width):
         span = slice(row, row + height), slice(column, column + width)
         return dh[span], dl[span]
@@ -125,35 +146,36 @@
         load.wait()
     for i in (3, 4, 5):
         prepare(i)
-        start = 384 - 128 * (i // 2)
-        m_send[1, i - 3 : i - 2, 0 : 512 - start] = window_mask(gm_s, i)[:, start:]
+        put_pattern(1, i)
+    m_send[1, 0:32] = pack(xp[4, :, 384:512])
 
     @pl.when(jnp.logical_not(replies))
     def _():
         pl.semaphore_wait(barrier, jnp.where(flat == 1, 1, 2))
 
-    for number in (0, 1, 2):
+    for number in range(4):
         sends[1][number].start()
     for i in (0, 1, 2):
         prepare(i)
-        m_send[0, i : i + 1, 128 * (i // 2) : 384] = window_mask(gm_s, i)[:, : 384 - 128 * (i // 2)]
+        put_pattern(0, i)
+    m_send[0, 0:32] = pack(xp[1, :, 0:128])
 
     @pl.when(jnp.logical_not(first_two))
     def _():
-        for number in (0, 1, 2):
+        for number in range(4):
             sends[0][number].start()
 
     to_right = product(d(384, 192, 128, 256), d(128, 256, 384, 256))
     p_send[1, 0:192] = to_right[:, :128]
-    p_send[1, 192:288] = to_right[0:96, 128:] + pltpu.roll(to_right[96:192, 128:], 64, 1)
-    sends[1][3].start()
+    p_send[1, 192:288] = pack(to_right[:, 128:])
+    sends[1][4].start()
     to_left = product(d(192, 192, 384, 256), d(384, 256, 128, 256))
     p_send[0, 0:192] = to_left[:, 128:]
-    p_send[0, 192:288] = to_left[0:96, :128] + pltpu.roll(to_left[96:192, :128], 64, 1)
+    p_send[0, 192:288] = pack(to_left[:, :128])
 
     @pl.when(jnp.logical_not(first_two))
     def _():
-        sends[0][3].start()
+        sends[0][4].start()
 
     for buffer in (gh, gl):
         buffer[...] = jnp.zeros_like(buffer)
@@ -171,32 +193,38 @@
             put_g(192 + 64 * i, 128 * p, value[64 * (i % 2) : 64 * (i % 2) + 64] * window_mask(gm_s, i))
 
     def take_x(side):
-        arrived(side, 0)
-        arrived(side, 1)
-        for r in range(3):
-            short = (r == 0) if side == 0 else (r == 2)
-            if side == 0:
-                value, column = (x_recv[0, r, :, 0:256] if short else x_recv[0, r]), 0
-            else:
-                value, column = (x_recv[1, r, :, 128:384], 512) if short else (x_recv[1, r], 384)
+        for number in range(4):
+            arrived(side, number)
+        half = unpack(m_recv[side, 0:32], side)
+        if side == 0:
+            values = [
+                (0, x_recv[0, 0, :, 0:256]),
+                (0, jnp.concatenate([x_recv[0, 1, :, 0:256], half], axis=1)),
+                (0, x_recv[0, 2]),
+            ]
+        else:
+            values = [
+                (384, x_recv[1, 0]),
+                (384, jnp.concatenate([half, x_recv[1, 1, :, 128:384]], axis=1)),
+                (512, x_recv[1, 2, :, 128:384]),
+            ]
+        for r, (column, value) in enumerate(values):
             high, rest = split(value)
             span = slice(64 * r + 576 * side, 64 * r + 576 * side + 64), slice(column, column + value.shape[1])
             dh[span] = high
             dl[span] = rest
 
     def take_p(side, halo):
-        arrived(side, 2)
-        arrived(side, 3)
+        arrived(side, 4)
         whole = p_recv[side, 0:192]
-        half = p_recv[side, 192:288]
-        half = jnp.concatenate([half, pltpu.roll(half, 64, 1)], axis=0)
-        if side == 0:
-            sums = [halo[:, 0:128] + whole, halo[:, 128:256] + jnp.where(low, half, 0.0), halo[:, 256:384]]
-        else:
-            sums = [halo[:, 0:128], halo[:, 128:256] + jnp.where(low, 0.0, half), halo[:, 256:384] + whole]
-        halo = jnp.concatenate(sums, axis=1)
+        half = unpack(p_recv[side, 192:288], side)
+        sums = [halo[:, 0:128], halo[:, 128:256] + half, halo[:, 256:384]]
+        sums[2 * side] += whole
         for r in range(3):
-            put_g(64 * r + 576 * side, 384 * side, halo[64 * r : 64 * r + 64] * m_recv[side, r : r + 1])
+            for t in range(3):
+                row = pattern_row(side, r, t)
+                if row is not None:
+                    put_g(64 * r + 576 * side, 384 * side + 128 * t, sums[t][64 * r : 64 * r + 64] * m_recv[side, row : row + 1])
 
     def finish(p, cubic):
         for i in (2 * p, 2 * p + 1):
@@ -242,7 +270,7 @@
         @pl.when(first_two)
         def _():
             pl.semaphore_wait(left_here, 1)
-            for number in range(4):
+            for number in range(5):
                 sends[0][number].start()
 
         edge, middle, halo = over(last)
@@ -293,12 +321,12 @@
             pltpu.VMEM((2, 3, BS, 384), F32),
             pltpu.VMEM((2, 288, 128), F32),
             pltpu.VMEM((2, 288, 128), F32),
-            pltpu.VMEM((2, 8, 384), F32),
-            pltpu.VMEM((2, 8, 384), F32),
+            pltpu.VMEM((2, 40, 128), F32),
+            pltpu.VMEM((2, 40, 128), F32),
             pltpu.VMEM((3, 128, 512), F32),
             pltpu.SemaphoreType.DMA((ROWS + 2,)),
-            pltpu.SemaphoreType.DMA((2, 4)),
-            pltpu.SemaphoreType.DMA((2, 4)),
+            pltpu.SemaphoreType.DMA((2, 5)),
+            pltpu.SemaphoreType.DMA((2, 5)),
             pltpu.SemaphoreType.REGULAR,
         ],
         compiler_params=pltpu.CompilerParams(

time: 17.6 us -> 17.4 us (0.989)
  Pallas kernels: 16.6 us -> 16.4 us
    pallas_call x1, Pallas kernels: 16.6 us -> 16.4 us  [body(): pl.pallas_call(kernel, out_shape=jax.ShapeDtypeStruct(x_band.shape, F32),...]
where the time goes in v4:
time: 17.4 us; the launch traced here: 17.3 us
  Pallas kernels  16.4 us (94%)
  local copies, waits for them, and re-layouts  0.88 us (5%)
    pallas_call x1, Pallas kernels, body(): pl.pallas_call(kernel, out_shape=jax.ShapeDtypeStruct(x_band.shape, F32),...  16.4 us
    unnamed x1, local copies, waits for them, and re-layouts  0.88 us

profile of v4, /device:TPU:0, one launch (start us, length us, event | category | flops | bytes accessed | tf_op | source)
XLA Modules:
  0.0 17.3 jit_solution(10991017447432465763)
XLA Ops:
  0.0 16.4 %shard_map.37 = f32[6,64,448]{2,1,0:T(8,128)S(1)} custom-call(f32[6,64,448]{2,1,0:T(8,128)} %x_hbm.1, s32[6,7]{1,0:T(8,128)} %xm_hbm.1, s32[6,7]{1,0:T(8,128)} %gm_hbm.1), custom_call_target="tpu_custom_call" | custom-call | flops 1000000000 | bytes 1500000 | tf_op jit(solution)/shard_map/pallas_call | solution.py:306
  16.4 0.9 %copy.5 = f32[6,64,448]{2,1,0:T(8,128)} copy(f32[6,64,448]{2,1,0:T(8,128)S(1)} %shard_map.37) | data formatting | bytes 1376256

commit v5 on v4

--- a/solution.py
+++ b/solution.py
@@ -26,8 +26,12 @@
     return jnp.dot(lhs, rhs, preferred_element_type=F32)
 
 
+def works_right_last(flat):
+    return jnp.logical_and(lax.rem(flat, 2) == 1, flat != 1)
+
+
 def kernel(
-    x_hbm, xm_hbm, gm_hbm, z_out,
+    x_hbm, xm_hbm, gm_hbm, done, part, scale, eh, el, hh, hl,
     x_v, xm_s, gm_s, xp, dh, dl, gh, gl, gacc, x_recv, p_send, p_recv, m_send, m_recv,
     zacc, in_sem, send_sem, recv_sem, left_here,
 ):
@@ -51,7 +55,7 @@
     mask_loads = [pltpu.make_async_copy(xm_hbm, xm_s, in_sem.at[ROWS]), pltpu.make_async_copy(gm_hbm, gm_s, in_sem.at[ROWS + 1])]
     for load in mask_loads:
         load.start()
-    for i in (3, 4, 5, 0, 1, 2):
+    for i in (5, 4, 3, 0, 1, 2):
         loads[i].start()
     for buffer in (dh, dl):
         buffer[...] = jnp.zeros_like(buffer)
@@ -144,17 +148,17 @@
 
     for load in mask_loads:
         load.wait()
-    for i in (3, 4, 5):
+
+    @pl.when(jnp.logical_not(replies))
+    def _():
+        pl.semaphore_wait(barrier, jnp.where(flat == 1, 1, 2))
+
+    for number, i in enumerate((5, 4, 3)):
         prepare(i)
+        sends[1][number].start()
         put_pattern(1, i)
     m_send[1, 0:32] = pack(xp[4, :, 384:512])
-
-    @pl.when(jnp.logical_not(replies))
-    def _():
-        pl.semaphore_wait(barrier, jnp.where(flat == 1, 1, 2))
-
-    for number in range(4):
-        sends[1][number].start()
+    sends[1][3].start()
     for i in (0, 1, 2):
         prepare(i)
         put_pattern(0, i)
@@ -214,7 +218,7 @@
             dh[span] = high
             dl[span] = rest
 
-    def take_p(side, halo):
+    def take_p(side, halo, put, place):
         arrived(side, 4)
         whole = p_recv[side, 0:192]
         half = unpack(p_recv[side, 192:288], side)
@@ -224,13 +228,24 @@
             for t in range(3):
                 row = pattern_row(side, r, t)
                 if row is not None:
-                    put_g(64 * r + 576 * side, 384 * side + 128 * t, sums[t][64 * r : 64 * r + 64] * m_recv[side, row : row + 1])
-
-    def finish(p, cubic):
+                    put(64 * r + place[0], 128 * t + place[1], sums[t][64 * r : 64 * r + 64] * m_recv[side, row : row + 1])
+
+    def put_h(row, column, value):
+        high, rest = split(value)
+        span = slice(row, row + 64), slice(column, column + 128)
+        hh[span] = high
+        hl[span] = rest
+
+    def finish(p, cubic, last):
         for i in (2 * p, 2 * p + 1):
             start = 64 * (i % 2)
-            z = 1.5 * xp[i] - (0.5 * window_mask(xm_s, i)) * cubic[start : start + 64]
-            z_out[i] = z[:, start : start + W * BS]
+            half = 0.5 * window_mask(xm_s, i)
+            z = 1.5 * xp[i] - half * cubic[start : start + 64]
+            if i // 3 == last:
+                part[i % 3] = z
+                scale[i % 3 : i % 3 + 1] = half
+            else:
+                done[i % 3] = z[:, start : start + W * BS]
 
     def over(side):
         take_x(side)
@@ -261,7 +276,7 @@
         edge, middle, halo = over(first)
         gacc[1, :, near] += middle
         put_pair(2 * first, gacc[2 * first] + edge)
-        take_p(first, halo + halo_over(first))
+        take_p(first, halo + halo_over(first), put_g, (576 * first, 384 * first))
         edge, middle = cubic_over(first)
         zacc[2 * first] = edge
         zacc[1] = jnp.zeros((128, 512), F32)
@@ -277,17 +292,21 @@
         put_pair(2 * last, gacc[2 * last] + edge)
         gacc[1, :, far] += middle
         put_pair(1, gacc[1])
+        finish(2 * first, zacc[2 * first] + cubic_within(2 * first), last)
+        edge, middle = cubic_over(last)
+        finish(2 * last, edge + cubic_within(2 * last), last)
+        zacc[1] += cubic_within(1)
+        zacc[1, :, far] += middle
+        finish(1, zacc[1], last)
         halo += halo_over(last)
-        finish(2 * first, zacc[2 * first] + cubic_within(2 * first))
-        zacc[2 * last] = cubic_within(2 * last)
-        zacc[1] += cubic_within(1)
-        take_p(last, halo)
-        edge, middle = cubic_over(last)
-        finish(2 * last, zacc[2 * last] + edge)
-        zacc[1, :, far] += middle
-        finish(1, zacc[1])
-
-    right_last = jnp.logical_and(lax.rem(flat, 2) == 1, flat != 1)
+        e = d(192 + 192 * last, 192, 512 * last, 256)
+        eh[...] = e[0]
+        el[...] = e[1]
+        for half in (hh, hl):
+            half[...] = jnp.zeros_like(half)
+        take_p(last, halo, put_h, (64 * last, 0))
+
+    right_last = works_right_last(flat)
 
     @pl.when(jnp.logical_not(right_last))
     def _():
@@ -302,12 +321,49 @@
             copy.wait_send()
 
 
+def closing(done, part, scale, eh, el, hh, hl, z_hbm, z_v, sem):
+    right_last = works_right_last(lax.axis_index("row") * lax.axis_size("col") + lax.axis_index("col"))
+
+    def write(last):
+        stores = [pltpu.make_async_copy(done, z_hbm.at[3 - 3 * last : 6 - 3 * last], sem.at[3])]
+        stores[0].start()
+        cubic = product((eh[...], el[...]), (hh[...], hl[...]))
+        for r in range(3):
+            i = 3 * last + r
+            shift = 128 * (3 * last - i // 2)
+            term = cubic[64 * r : 64 * r + 64]
+            if shift < 0:
+                term = jnp.concatenate([term[:, -shift:], jnp.zeros((BS, 128 - shift), F32)], axis=1)
+            elif shift == 0:
+                term = jnp.concatenate([term, jnp.zeros((BS, 128), F32)], axis=1)
+            else:
+                term = jnp.concatenate([jnp.zeros((BS, shift), F32), term[:, : 512 - shift]], axis=1)
+            z = part[r] - scale[r : r + 1] * term
+            z_v[r] = z[:, 64 * (i % 2) : 64 * (i % 2) + W * BS]
+            stores.append(pltpu.make_async_copy(z_v.at[r], z_hbm.at[i], sem.at[r]))
+            stores[-1].start()
+        for store in stores:
+            store.wait()
+
+    @pl.when(jnp.logical_not(right_last))
+    def _():
+        write(0)
+
+    @pl.when(right_last)
+    def _():
+        write(1)
+
+
 def body(x_band, x_mask, g_mask):
-    return pl.pallas_call(
+    shapes = [
+        ((3, BS, W * BS), F32), ((3, BS, 512), F32), ((8, 512), F32),
+        ((192, 256), BF16), ((192, 256), BF16), ((256, 384), BF16), ((256, 384), BF16),
+    ]
+    between = pl.pallas_call(
         kernel,
-        out_shape=jax.ShapeDtypeStruct(x_band.shape, F32),
+        out_shape=[jax.ShapeDtypeStruct(*shape) for shape in shapes],
         in_specs=[pl.BlockSpec(memory_space=pltpu.HBM)] * 3,
-        out_specs=pl.BlockSpec(memory_space=pltpu.VMEM),
+        out_specs=[pl.BlockSpec(memory_space=pltpu.VMEM)] * len(shapes),
         scratch_shapes=[
             pltpu.VMEM((ROWS, BS, W * BS), F32),
             pltpu.SMEM((ROWS, W), jnp.int32),
@@ -334,6 +390,14 @@
         ),
         cost_estimate=pl.CostEstimate(flops=1_000_000_000, bytes_accessed=1_500_000, transcendentals=0),
     )(*(pltpu.with_memory_space_constraint(a, pltpu.HBM) for a in (x_band, x_mask, g_mask)))
+    return pl.pallas_call(
+        closing,
+        out_shape=jax.ShapeDtypeStruct(x_band.shape, F32),
+        in_specs=[pl.BlockSpec(memory_space=pltpu.VMEM)] * len(shapes),
+        out_specs=pl.BlockSpec(memory_space=pltpu.HBM),
+        scratch_shapes=[pltpu.VMEM((3, BS, W * BS), F32), pltpu.SemaphoreType.DMA((4,))],
+        compiler_params=pltpu.CompilerParams(vmem_limit_bytes=16 * 1024 * 1024),
+    )(*(pltpu.with_memory_space_constraint(a, pltpu.VMEM) for a in between))
 
 
 def solution(mesh):

time: 17.4 us -> 17.1 us (0.983)
  local copies, waits for them, and re-layouts: 0.88 us -> 0 us
  Pallas kernels: 16.4 us -> 17 us
    unnamed x1 -> x0, local copies, waits for them, and re-layouts: 0.88 us -> none
    pallas_call x1 -> x2, Pallas kernels: 16.4 us -> 17 us  [the longest x1 15.8 us: body(): pl.pallas_call(kernel, out_shape=[jax.ShapeDtypeStruct(*shape) for shape...]
where the time goes in v5:
time: 17.1 us; the launch traced here: 17 us
  Pallas kernels  17 us (99%)
    pallas_call x1, Pallas kernels, body(): pl.pallas_call(kernel, out_shape=[jax.ShapeDtypeStruct(*shape) for shape...  15.8 us
    pallas_call x1, Pallas kernels, body(): pl.pallas_call(closing, out_shape=jax.ShapeDtypeStruct(x_band.shape, F32)...  1.13 us

profile of v5, /device:TPU:0, one launch (start us, length us, event | category | flops | bytes accessed | tf_op | source)
XLA Modules:
  0.0 17.0 jit_solution(14627321407906805034)
XLA Ops:
  0.0 15.8 %shard_map.37 = (f32[3,64,448]{2,1,0:T(8,128)S(1)}, f32[3,64,512]{2,1,0:T(8,128)S(1)}, f32[8,512]{1,0:T(8,128)S(1)}, bf16[192,256]{1,0:T(8,128)(2,1)S(1)}, bf16[...) custom-call(f32[6,64,448]{2,1,0:T(8,128)} %x_hbm.1, s32[6,7]{1,0:T(8,128)} %xm_hbm.1, ...), custom_call_target="tpu_custom_call" | custom-call | flops 1000000000 | bytes 1500000 | tf_op jit(solution)/shard_map/pallas_call | solution.py:362
  15.8 1.1 %shard_map.38 = f32[6,64,448]{2,1,0:T(8,128)} custom-call(f32[3,64,448]{2,1,0:T(8,128)S(1)} %get-tuple-element.12.done, f32[3,64,512]{2,1,0:T(8,128)S(1)} %get-tuple-element.13.part, f32[8,512]{1,0:T(8,128)S(1)} %get-tuple-element.14.scale, bf16[192,256]{1,0:T(8,128)(2,1)S(1)} %get-tuple-element.15.eh, bf16[192,256]{1,0:T(8,128)(2,1)S(1)} %get-tuple-element.16.el, ...), custom_call_target="tpu_custom_call" | custom-call | tf_op jit(solution)/shard_map/pallas_call | solution.py:393

commit v6 on v5

--- a/solution.py
+++ b/solution.py
@@ -181,7 +181,7 @@
     def _():
         sends[0][4].start()
 
-    for buffer in (gh, gl):
+    for buffer in (gh, gl, hh, hl):
         buffer[...] = jnp.zeros_like(buffer)
     for p in range(3):
         gacc[p] = product(d(192 + 128 * p, 128, 256, 256), d(256, 256, 128 * p, 512))
@@ -256,9 +256,10 @@
         return outer[128:256], outer[0:128, 0:384], outer[256:448, 128:512]
 
     def halo_over(side):
+        none = jnp.zeros((64, 384), F32)
         if side == 0:
-            return product(d(0, 192, 256, 256), d(256, 256, 0, 384))
-        return product(d(576, 192, 256, 256), d(256, 256, 384, 384))
+            return jnp.concatenate([none, product(d(64, 128, 256, 128), d(256, 128, 0, 384))], axis=0)
+        return jnp.concatenate([product(d(576, 128, 384, 128), d(384, 128, 384, 384)), none], axis=0)
 
     def cubic_over(side):
         if side == 0:
@@ -302,8 +303,6 @@
         e = d(192 + 192 * last, 192, 512 * last, 256)
         eh[...] = e[0]
         el[...] = e[1]
-        for half in (hh, hl):
-            half[...] = jnp.zeros_like(half)
         take_p(last, halo, put_h, (64 * last, 0))
 
     right_last = works_right_last(flat)

time: 17.1 us -> 17.1 us (level)
  no operation moved by 1% of the time
where the time goes in v6:
time: 17.1 us; the launch traced here: 17 us
  Pallas kernels  17 us (99%)
    pallas_call x1, Pallas kernels, body(): pl.pallas_call(kernel, out_shape=[jax.ShapeDtypeStruct(*shape) for shape...  15.8 us
    pallas_call x1, Pallas kernels, body(): pl.pallas_call(closing, out_shape=jax.ShapeDtypeStruct(x_band.shape, F32)...  1.13 us

profile of v6, /device:TPU:0, one launch (start us, length us, event | category | flops | bytes accessed | tf_op | source)
XLA Modules:
  0.0 17.0 jit_solution(8734294468788121123)
XLA Ops:
  0.0 15.8 %shard_map.37 = (f32[3,64,448]{2,1,0:T(8,128)S(1)}, f32[3,64,512]{2,1,0:T(8,128)S(1)}, f32[8,512]{1,0:T(8,128)S(1)}, bf16[192,256]{1,0:T(8,128)(2,1)S(1)}, bf16[...) custom-call(f32[6,64,448]{2,1,0:T(8,128)} %x_hbm.1, s32[6,7]{1,0:T(8,128)} %xm_hbm.1, ...), custom_call_target="tpu_custom_call" | custom-call | flops 1000000000 | bytes 1500000 | tf_op jit(solution)/shard_map/pallas_call | solution.py:361
  15.8 1.1 %shard_map.38 = f32[6,64,448]{2,1,0:T(8,128)} custom-call(f32[3,64,448]{2,1,0:T(8,128)S(1)} %get-tuple-element.12.done, f32[3,64,512]{2,1,0:T(8,128)S(1)} %get-tuple-element.13.part, f32[8,512]{1,0:T(8,128)S(1)} %get-tuple-element.14.scale, bf16[192,256]{1,0:T(8,128)(2,1)S(1)} %get-tuple-element.15.eh, bf16[192,256]{1,0:T(8,128)(2,1)S(1)} %get-tuple-element.16.el, ...), custom_call_target="tpu_custom_call" | custom-call | tf_op jit(solution)/shard_map/pallas_call | solution.py:392
